TPU v7x, 32 devices: a whole 2x2x4 slice. The times are simulated.
32 devices in a mesh: case: 2 (over y), wall: 4 (over z), azim: 4 (over x, core).
Axes of the slice: x: 2, y: 2, z: 4, core: 2. Of those that a mesh axis runs over, the one named last changes fastest.
Arguments:
- state: float32 [12, 2, 32, 512], P(None, 'case', 'wall', 'azim'), parts along dimension 1, may hold values from 0.5 to 1.5
- courant: float32 [2, 32, 512], P('case', 'wall', 'azim'), parts along dimension 0, may hold values from -0.6 to 0.6
- cross_sections: float32 [64], replicated, may hold values from 0.02 to 0.6
- band_fractions: float32 [64], replicated, may hold values from 0.02 to 0.2
- absorb_index: int32 [11, 16], replicated, may hold values from 0 to 63
- band_index: int32 [16], replicated, may hold values from 0 to 63
Outputs:
- new_state: float32 [12, 2, 32, 512], P(None, 'case', 'wall', 'azim'), parts along dimension 1
- wall_flux: float32 [2, 512], P('case', 'azim'), parts along dimension 0
There are 2 independent parts, one for each index of `case`. A program takes and returns all parts, laid end to end along the dimension named above; an argument that names none is the same for every part. Nothing has to cross between parts.
All inputs are finite; a program needn't handle non-finite values.
Results may differ from a plain program's by a relative error of at most 0.0003.
Values sent between devices are 32-bit elements; how exact they have to be, the bound alone decides.
A program may use at most 64 MiB of HBM per device.

v0:
```python
import functools

import jax
import jax.numpy as jnp
from jax import lax
from jax.experimental import pallas as pl
from jax.experimental.pallas import tpu as pltpu
from jax.sharding import PartitionSpec as P

WEIGHTS = (0.55, 0.45)
RATES = (1.15, 3.4)
FILTER = 0.02
COUPLING = 0.1
REACH = 6
MESH = pl.DeviceIdType.MESH
EXACT = lax.Precision.HIGHEST


def loop(count, body, init):
    if count <= 4:
        for i in range(count):
            init = body(i, init)
        return init
    return lax.fori_loop(0, count, body, init)


def kernel(
    walls, azims, state, courant, sections, fractions, absorb, band,
    new_state, wall_out,
    gs, gc, gl, gr, gh, ms, mh, edge_l, edge_r, em, t1, t2, net, net_h, mat,
    table, idx, cs, bf, bi,
    local_sem, edge_sem, s_state, r_state, s_cour, r_cour,
):
    comps, rows, lanes = state.shape
    species, bands = absorb.shape
    entries = sections.shape[0]
    total = rows * walls
    me = lax.axis_index("wall")
    az = lax.axis_index("azim")
    right, left = lax.rem(az + 1, azims), lax.rem(az + azims - 1, azims)

    def peer(d):
        return lax.rem(me + d, walls)

    def source(d):
        return lax.rem(me + walls - d, walls)

    barrier = pltpu.get_barrier_semaphore()

    def greet(i, _):
        pl.semaphore_signal(barrier, inc=1, device_id={"wall": peer(i + 1)}, device_id_type=MESH)
        return 0

    loop(walls - 1, greet, 0)
    for side in (left, right):
        pl.semaphore_signal(barrier, inc=1, device_id={"azim": side}, device_id_type=MESH)

    loads = [
        pltpu.make_async_copy(src, dst, local_sem.at[i])
        for i, (src, dst) in enumerate(
            [(state, gs.at[me]), (courant, gc.at[me, 0]), (sections, cs), (fractions, bf), (absorb, idx), (band, bi)]
        )
    ]
    for c in loads:
        c.start()
    lane = lax.broadcasted_iota(jnp.int32, (rows, lanes), 1)

    pl.semaphore_wait(barrier, walls + 1)

    def state_copy(d, slot):
        return pltpu.make_async_remote_copy(
            src_ref=state, dst_ref=gs.at[slot], send_sem=s_state.at[d], recv_sem=r_state.at[d],
            device_id={"wall": peer(d)}, device_id_type=MESH)

    def line_copy(d, slot):
        return pltpu.make_async_remote_copy(
            src_ref=gc.at[me], dst_ref=gc.at[slot], send_sem=s_cour.at[d], recv_sem=r_cour.at[d],
            device_id={"wall": peer(d)}, device_id_type=MESH)

    def send_state(i, _):
        state_copy(i + 1, me).start()
        return 0

    def send_line(i, _):
        line_copy(i + 1, me).start()
        return 0

    loop(walls - 1, send_state, 0)

    for c in loads[:2]:
        c.wait()
    el = jnp.zeros((rows, lanes), jnp.float32)
    er = jnp.zeros((rows, lanes), jnp.float32)
    for c in range(comps + 1):
        x = gs[me, c] if c < comps else gc[me, 0]
        here = (lane >= REACH * c) & (lane < REACH * (c + 1))
        el = jnp.where(here, pltpu.roll(x, REACH * c, 1) if c else x, el)
        er = jnp.where(here, pltpu.roll(x, (REACH * (c + 1)) % lanes, 1), er)
    edge_l[...] = el
    edge_r[...] = er

    edges = [
        pltpu.make_async_remote_copy(
            src_ref=src, dst_ref=dst, send_sem=edge_sem.at[2 * i], recv_sem=edge_sem.at[2 * i + 1],
            device_id={"azim": to}, device_id_type=MESH)
        for i, (src, dst, to) in enumerate([(edge_r, gl, right), (edge_l, gr, left)])
    ]
    for c in edges:
        c.start()

    for c in loads[2:]:
        c.wait()
    index = idx[...]
    picked = lax.fori_loop(
        0, entries, lambda t, acc: jnp.where(index == t, cs[t], acc), jnp.zeros((species, bands), jnp.float32), unroll=8)
    table[...] = jnp.zeros_like(table)
    table[0:species, 0:bands] = picked
    kpad = table.shape[0]
    rb = rows * bands
    spread = jnp.where(
        lax.broadcasted_iota(jnp.int32, (rb, lanes), 0) & (bands - 1) == lax.broadcasted_iota(jnp.int32, (rb, lanes), 1), 1.0, 0.0)
    by_row = lax.dot_general(spread, table[...], (((1,), (1,)), ((), ())), precision=EXACT, preferred_element_type=jnp.float32)
    cr = comps * rows
    columns = jnp.where(
        lax.broadcasted_iota(jnp.int32, (kpad, cr), 1) // rows == lax.broadcasted_iota(jnp.int32, (kpad, cr), 0) + 1, 1.0, 0.0)
    full = jnp.dot(by_row, columns, precision=EXACT, preferred_element_type=jnp.float32)
    same_row = lax.broadcasted_iota(jnp.int32, (rb, cr), 0) // bands == lax.broadcasted_iota(jnp.int32, (rb, cr), 1) % rows
    mat[...] = jnp.where(same_row, full, 0.0) * (1.0 / total)
    band_row = lax.broadcasted_iota(jnp.int32, (bands, lanes), 0)
    share = jnp.zeros((bands, lanes), jnp.float32)
    for b in range(bands):
        share = jnp.where(band_row == b, bf[bi[b]], share)
    diff_r = lax.broadcasted_iota(jnp.int32, (rows, (rows + 2) * 8), 1) // 8
    diff_i = lax.broadcasted_iota(jnp.int32, (rows, (rows + 2) * 8), 0)
    diff = jnp.where(diff_r == diff_i, 1.0, 0.0) - jnp.where(diff_r == diff_i + 2, 1.0, 0.0)
    heat_scale = COUPLING * total / 2.0

    def cells(ref, z):
        u = ref[z][0:comps].reshape(cr, lanes)
        step = jnp.dot(mat[...], u, precision=EXACT, preferred_element_type=jnp.float32)
        t = ref[z, 0]
        t = t * t
        t = t * t
        t1[z] = jnp.exp(step * (-0.5 * RATES[0]))
        t2[z] = jnp.exp(step * (-0.5 * RATES[1]))
        for r in range(rows):
            part = slice(r * bands, (r + 1) * bands)
            em[z, part] = step[part] * (share * t[r : r + 1])

    def scan(out):
        zero = jnp.zeros((bands, lanes), jnp.float32)

        def fold(a):
            s = a[0:8]
            for k in range(8, bands, 8):
                s = s + a[k : k + 8]
            return s

        def up(z, carry):
            u1, u2, a1, a2 = carry
            for r in range(rows):
                part = slice(r * bands, (r + 1) * bands)
                e, b1, b2 = em[z, part], t1[z, part], t2[z, part]
                u1 = WEIGHTS[0] * e + (a1 * b1) * u1
                u2 = WEIGHTS[1] * e + (a2 * b2) * u2
                out[1 + z * rows + r] = fold(u1 + u2)
                a1, a2 = b1, b2
            return u1, u2, a1, a2

        def down(i, carry):
            d1, d2, a1, a2 = carry
            z = walls - 1 - i
            for r in reversed(range(rows)):
                part = slice(r * bands, (r + 1) * bands)
                e, b1, b2 = em[z, part], t1[z, part], t2[z, part]
                d1 = WEIGHTS[0] * e + (a1 * b1) * d1
                d2 = WEIGHTS[1] * e + (a2 * b2) * d2
                at = 1 + z * rows + r
                out[at] = out[at] - fold(d1 + d2)
                a1, a2 = b1, b2
            return d1, d2, a1, a2

        loop(walls, up, (zero, zero, zero, zero))
        d1, d2, a1, a2 = loop(walls, down, (zero, zero, zero, zero))
        out[0] = out[1]
        out[total + 1] = out[total]
        return jnp.sum(fold(a1 * d1 + a2 * d2), axis=0, keepdims=True)

    def heat(ref, z):
        part = ref[pl.ds(z * rows, rows + 2)].reshape((rows + 2) * 8, lanes)
        return heat_scale * jnp.dot(diff, part, precision=EXACT, preferred_element_type=jnp.float32)

    def shifts(x, h):
        own, halo = {0: x}, {0: h}
        for o in (1, 2, 3, -1, -2, -3):
            rx, rh = pltpu.roll(x, (-o) % lanes, 1), pltpu.roll(h, (-o) % lanes, 1)
            inside = lane < lanes - o if o > 0 else lane >= -o
            own[o] = jnp.where(inside, rx, rh)
            halo[o] = jnp.where(inside, rh, rx)
        return own, halo

    def tendency(s, cour):
        gradient = (45.0 / 60.0) * (s[1] - s[-1]) - (9.0 / 60.0) * (s[2] - s[-2]) + (1.0 / 60.0) * (s[3] - s[-3])
        smooth = (s[-3] + s[3]) - 6.0 * (s[-2] + s[2]) + 15.0 * (s[-1] + s[1]) - 20.0 * s[0]
        return FILTER * smooth - cour * gradient

    def unpack(z, pr, pk):
        for c in range(comps + 1):
            a = pltpu.roll(pr, lanes - REACH * c, 1) if c else pr
            b = pltpu.roll(pk, lanes - REACH * (c + 1), 1)
            gh[z, c] = jnp.where(lane < lanes // 2, a, b)
        cells(gh, z)

    cells(gs, me)
    for c in edges:
        c.wait_recv()
    gc[me, 1] = jnp.where(lane % REACH < REACH // 2, gr[...], gl[...])
    loop(walls - 1, send_line, 0)

    def arrive(i, _):
        z = source(i + 1)
        state_copy(i + 1, z).wait_recv()
        cells(gs, z)
        return 0

    loop(walls - 1, arrive, 0)
    flux = scan(net)
    unpack(me, gr[...], gl[...])

    def halos(i, _):
        z = source(i + 1)
        line_copy(i + 1, z).wait_recv()
        packed = gc[z, 1]
        unpack(z, packed, packed)
        return 0

    loop(walls - 1, halos, 0)
    scan(net_h)

    def middle(z, _):
        cour = gc[z, 0]
        for c in range(comps):
            x = gs[z, c]
            own, _h = shifts(x, gh[z, c])
            change = tendency(own, cour)
            if c == 0:
                change = change + heat(net, z)
            ms[z, c] = x + change
        cells(ms, z)
        return 0

    loop(walls, middle, 0)
    flux = flux + scan(net)
    wall_out[...] = 0.5 * flux
    hc = gh[me, comps]
    for c in range(comps):
        h = gh[me, c]
        _o, halo = shifts(gs[me, c], h)
        change = tendency(halo, hc)
        if c == 0:
            change = change + heat(net_h, me)
        mh[c] = h + change

    cour = gc[me, 0]
    for c in range(comps):
        x = ms[me, c]
        own, _h = shifts(x, mh[c])
        change = tendency(own, cour)
        if c == 0:
            change = change + heat(net, me)
        new_state[c] = 0.5 * (gs[me, c] + x + change)

    def finish(i, _):
        state_copy(i + 1, me).wait_send()
        line_copy(i + 1, me).wait_send()
        return 0

    loop(walls - 1, finish, 0)
    for c in edges:
        c.wait_send()


def hand_over(a, b, a_out, b_out, sems):
    copies = [pltpu.make_async_copy(a, a_out, sems.at[0]), pltpu.make_async_copy(b, b_out, sems.at[1])]
    for c in copies:
        c.start()
    for c in copies:
        c.wait()


def local(walls, azims, state, courant, cross_sections, band_fractions, absorb_index, band_index):
    comps, stations, rows, lanes = state.shape
    bands = absorb_index.shape[1]
    species = absorb_index.shape[0]
    entries = cross_sections.shape[0]
    total = rows * walls
    f32 = jnp.float32
    vmem = pltpu.VMEM
    dma = pltpu.SemaphoreType.DMA
    hbm_spec = pl.BlockSpec(memory_space=pltpu.HBM)
    vmem_spec = pl.BlockSpec(memory_space=pltpu.VMEM)
    new_state, wall = pl.pallas_call(
        functools.partial(kernel, walls, azims),
        out_shape=(
            pltpu.VMEM((comps, rows, lanes), f32),
            pltpu.VMEM((1, lanes), f32),
        ),
        in_specs=[hbm_spec] * 6,
        out_specs=(vmem_spec, vmem_spec),
        scratch_shapes=[
            vmem((walls, comps, rows, lanes), f32),
            vmem((walls, 2, rows, lanes), f32),
            vmem((rows, lanes), f32),
            vmem((rows, lanes), f32),
            vmem((walls, comps + 1, rows, lanes), f32),
            vmem((walls, comps, rows, lanes), f32),
            vmem((comps, rows, lanes), f32),
            vmem((rows, lanes), f32),
            vmem((rows, lanes), f32),
            vmem((walls, rows * bands, lanes), f32),
            vmem((walls, rows * bands, lanes), f32),
            vmem((walls, rows * bands, lanes), f32),
            vmem((total + 2, 8, lanes), f32),
            vmem((total + 2, 8, lanes), f32),
            vmem((rows * bands, comps * rows), f32),
            vmem((16, lanes), f32),
            vmem((species, bands), jnp.int32),
            pltpu.SMEM((entries,), f32),
            pltpu.SMEM((entries,), f32),
            pltpu.SMEM((bands,), jnp.int32),
            dma((6,)),
            dma((4,)),
        ] + [dma((walls,))] * 4,
        compiler_params=pltpu.CompilerParams(
            collective_id=0, has_side_effects=True, vmem_limit_bytes=58 * 1024 * 1024),
    )(state.reshape(comps, rows, lanes), courant.reshape(rows, lanes), cross_sections, band_fractions, absorb_index, band_index)
    hbm = pl.BlockSpec(memory_space=pltpu.HBM)
    new_state, wall = pl.pallas_call(
        hand_over,
        out_shape=(
            jax.ShapeDtypeStruct((comps, rows, lanes), f32),
            jax.ShapeDtypeStruct((1, lanes), f32),
        ),
        in_specs=[pl.BlockSpec(memory_space=pl.ANY)] * 2,
        out_specs=(hbm, hbm),
        scratch_shapes=[dma((2,))],
    )(pltpu.with_memory_space_constraint(new_state, pltpu.VMEM), pltpu.with_memory_space_constraint(wall, pltpu.VMEM))
    return new_state.reshape(state.shape), wall


def solution(mesh):
    return jax.shard_map(
        functools.partial(local, mesh.shape["wall"], mesh.shape["azim"]),
        mesh=mesh,
        in_specs=(P(None, "case", "wall", "azim"), P("case", "wall", "azim"), P(), P(), P(), P()),
        out_specs=(P(None, "case", "wall", "azim"), P("case", "azim")),
        check_vma=False,
    )
```

profile of v0, /device:TPU:0, one launch (start us, length us, event | category | flops | bytes accessed | tf_op | source)
XLA Modules:
  0.0 14.9 jit_solution(14471878367388950500)
XLA Ops:
  0.6 13.6 %shard_map.77 = (f32[12,8,128]{2,1,0:T(8,128)S(1)}, f32[1,128]{1,0:T(1,128)S(1)}) custom-call(f32[12,8,128]{2,1,0:T(8,128)} %bitcast.5, f32[8,128]{1,0:T(8,128)} %bitcast.6, f32[64]{0:T(128)} %sections.1, f32[64]{0:T(128)} %fractions.1, s32[11,16]{1,0:T(8,128)} %absorb.1, s32[16]{0:T(128)} %band.1), custom_call_target="tpu_custom_call" | custom-call | tf_op jit(solution)/shard_map/pallas_call | solution.py:302
  14.2 0.6 %shard_map.78 = (f32[12,8,128]{2,1,0:T(8,128)}, f32[1,128]{1,0:T(1,128)}) custom-call(f32[12,8,128]{2,1,0:T(8,128)S(1)} %get-tuple-element.6.a, f32[1,128]{1,0:T(1,128)S(1)} %get-tuple-element.7.b), custom_call_target="tpu_custom_call" | custom-call | tf_op jit(solution)/shard_map/pallas_call | solution.py:338
where the time goes:
time: 15 us; the launch traced here: 14.9 us
  Pallas kernels  14.2 us (95%)
  between operations  0.64 us (4%)
    pallas_call x1, Pallas kernels, local(): pl.pallas_call(functools.partial(kernel, walls, azims), out_shape=(pltpu....  13.6 us
    pallas_call x1, Pallas kernels, local(): pl.pallas_call(hand_over, out_shape=(jax.ShapeDtypeStruct((comps, rows, l...  0.64 us

commit v1 on v0

v1 whole, which is shorter than its diff:
```python
import functools

import jax
import jax.numpy as jnp
from jax import lax
from jax.experimental import pallas as pl
from jax.experimental.pallas import tpu as pltpu
from jax.sharding import PartitionSpec as P

WEIGHTS = (0.55, 0.45)
RATES = (1.15, 3.4)
FILTER = 0.02
COUPLING = 0.1
REACH = 6
MESH = pl.DeviceIdType.MESH
EXACT = lax.Precision.HIGHEST


def loop(count, body, init):
    if count <= 4:
        for i in range(count):
            init = body(i, init)
        return init
    return lax.fori_loop(0, count, body, init)


def kernel(
    walls, azims, state, courant, sections, fractions, absorb, band,
    new_state, wall_out,
    gs, gc, gl, gr, ms, mh, edge_l, edge_r,
    em, t1, t2, em_h, t1_h, t2_h, em_m, t1_m, t2_m, net, net_h,
    table, idx, cs, bf, bi,
    local_sem, s_state, r_state, s_cour, r_cour, s_edge, r_edge, ready,
):
    comps, rows, lanes = state.shape
    species, bands = absorb.shape
    entries = sections.shape[0]
    total = rows * walls
    f32, bf16 = jnp.float32, jnp.bfloat16
    me = lax.axis_index("wall")
    az = lax.axis_index("azim")
    right, left = lax.rem(az + 1, azims), lax.rem(az + azims - 1, azims)
    sides = (right, left)
    first = ((az == azims - 1) | (az % 2 == 0), (left % 2 == 1) & (left != azims - 1))

    def peer(d):
        return lax.rem(me + d, walls)

    barrier = pltpu.get_barrier_semaphore()

    def greet(i, _):
        z = peer(i + 1)

        @pl.when(z > me)
        def _later():
            pl.semaphore_signal(barrier, inc=1, device_id={"wall": z}, device_id_type=MESH)
            for side in sides:
                pl.semaphore_signal(barrier, inc=1, device_id={"wall": z, "azim": side}, device_id_type=MESH)

        return 0

    loop(walls - 1, greet, 0)
    for i in range(2):

        @pl.when(jnp.logical_not(first[i]))
        def _later():
            pl.semaphore_signal(barrier, inc=1, device_id={"azim": sides[i]}, device_id_type=MESH)

    loads = [
        pltpu.make_async_copy(src, dst, local_sem.at[i])
        for i, (src, dst) in enumerate(
            [(state, gs.at[me]), (courant, gc.at[me]), (sections, cs), (fractions, bf), (absorb, idx), (band, bi)]
        )
    ]
    for c in loads:
        c.start()

    greeters = 3 * me + first[0].astype(jnp.int32) + first[1].astype(jnp.int32)

    @pl.when(greeters > 0)
    def _greeted():
        pl.semaphore_wait(barrier, greeters)


    def state_copy(d, slot):
        return pltpu.make_async_remote_copy(
            src_ref=state, dst_ref=gs.at[slot], send_sem=s_state.at[d], recv_sem=r_state.at[d],
            device_id={"wall": peer(d)}, device_id_type=MESH)

    def line_copy(d, slot):
        return pltpu.make_async_remote_copy(
            src_ref=courant, dst_ref=gc.at[slot], send_sem=s_cour.at[d], recv_sem=r_cour.at[d],
            device_id={"wall": peer(d)}, device_id_type=MESH)

    def edge_copy(i, d, slot):
        src, dst = ((edge_r, gl), (edge_l, gr))[i]
        return pltpu.make_async_remote_copy(
            src_ref=src, dst_ref=dst.at[slot], send_sem=s_edge.at[i, d], recv_sem=r_edge.at[i, d],
            device_id={"wall": peer(d), "azim": sides[i]}, device_id_type=MESH)

    def edge_copies(d, slot):
        return [edge_copy(i, d, slot) for i in range(2)]

    def state_first(i, _):
        z = peer(i + 1)

        @pl.when((z < me) & (z == 0))
        def _earliest():
            state_copy(i + 1, me).start()
            line_copy(i + 1, me).start()

        return 0

    def say_ready(i, _):
        z = peer(i + 1)

        @pl.when(z < me)
        def _earlier():
            pl.semaphore_signal(ready.at[0, me], inc=1, device_id={"wall": z}, device_id_type=MESH)
            for k, side in enumerate(sides):
                pl.semaphore_signal(ready.at[2 - k, me], inc=1, device_id={"wall": z, "azim": side}, device_id_type=MESH)

        return 0

    def rest_back(i, _):
        z = peer(i + 1)

        @pl.when((z < me) & (z > 0))
        def _earlier():
            state_copy(i, me).wait_send()
            state_copy(i + 1, me).start()
            line_copy(i + 1, me).start()

        @pl.when(z < me)
        def _edges():
            for c in edge_copies(i + 1, me):
                c.start()

        return 0

    def send_on(i, _):
        z = peer(i + 1)

        @pl.when(z > me)
        def _later():
            pl.semaphore_wait(ready.at[0, z], 1)
            state_copy(i + 1, me).start()
            line_copy(i + 1, me).start()
            for k in range(2):
                pl.semaphore_wait(ready.at[1 + k, z], 1)
                edge_copy(k, i + 1, me).start()

        return 0

    loop(walls - 1, state_first, 0)
    loop(walls - 1, say_ready, 0)
    for i in range(2):

        @pl.when(first[i])
        def _earlier():
            pl.semaphore_signal(ready.at[2 - i, me], inc=1, device_id={"azim": sides[i]}, device_id_type=MESH)

    for c in loads[:2]:
        c.wait()
    lane = lax.broadcasted_iota(jnp.int32, (rows, lanes), 1)
    el = jnp.zeros((rows, lanes), f32)
    er = jnp.zeros((rows, lanes), f32)
    for c in range(comps + 1):
        x = gs[me, c] if c < comps else gc[me]
        here = (lane >= REACH * c) & (lane < REACH * (c + 1))
        el = jnp.where(here, pltpu.roll(x, REACH * c, 1) if c else x, el)
        er = jnp.where(here, pltpu.roll(x, (REACH * (c + 1)) % lanes, 1), er)
    edge_l[...] = el
    edge_r[...] = er
    loop(walls - 1, rest_back, 0)
    for i in range(2):

        @pl.when(first[i])
        def _earlier():
            edge_copy(i, 0, me).start()


    for c in loads[2:]:
        c.wait()
    index = idx[...]
    picked = lax.fori_loop(
        0, entries, lambda t, acc: jnp.where(index == t, cs[t], acc), jnp.zeros((species, bands), f32), unroll=8)
    table[...] = jnp.zeros_like(table)
    table[0:species, 0:bands] = picked
    kpad = table.shape[0]
    rb = rows * bands
    cr = comps * rows
    spread = jnp.where(
        lax.broadcasted_iota(jnp.int32, (rb, lanes), 0) & (bands - 1) == lax.broadcasted_iota(jnp.int32, (rb, lanes), 1), 1.0, 0.0)
    by_row = lax.dot_general(spread, table[...], (((1,), (1,)), ((), ())), precision=EXACT, preferred_element_type=f32)
    columns = jnp.where(
        lax.broadcasted_iota(jnp.int32, (kpad, cr), 1) // rows == lax.broadcasted_iota(jnp.int32, (kpad, cr), 0) + 1, 1.0, 0.0)
    full = jnp.dot(by_row, columns, precision=EXACT, preferred_element_type=f32)
    same_row = lax.broadcasted_iota(jnp.int32, (rb, cr), 0) // bands == lax.broadcasted_iota(jnp.int32, (rb, cr), 1) % rows
    mat = jnp.where(same_row, full, 0.0) * (1.0 / total)
    mat_hi = mat.astype(bf16)
    mat_lo = (mat - mat_hi.astype(f32)).astype(bf16)
    mats = jnp.concatenate(
        [jnp.concatenate([mat_hi, mat_hi], axis=1), jnp.concatenate([mat_lo, mat_lo], axis=1)], axis=0)
    band_row = lax.broadcasted_iota(jnp.int32, (bands, lanes), 0)
    share = jnp.zeros((bands, lanes), f32)
    for b in range(bands):
        share = jnp.where(band_row == b, bf[bi[b]], share)
    share = share * WEIGHTS[0]
    heat_scale = COUPLING * total / 2.0

    def steps(values):
        u = values.reshape(cr, lanes)
        hi = u.astype(bf16)
        lo = (u - hi.astype(f32)).astype(bf16)
        both = jnp.dot(mats, jnp.concatenate([hi, lo], axis=0), preferred_element_type=f32)
        return both[:rb] + both[rb:]

    def fill(z, values, to_em, to_1, to_2, hot):
        step = steps(values)
        to_1[z] = jnp.exp(step * (-0.5 * RATES[0]))
        to_2[z] = jnp.exp(step * (-0.5 * RATES[1]))
        if hot:
            t = fourth(values[0])
        for r in range(rows):
            part = slice(r * bands, (r + 1) * bands)
            to_em[z, part] = step[part] * (share * t[r : r + 1] if hot else share)

    def fourth(t):
        t = t * t
        return t * t

    def fold(a):
        s = a[0:8]
        for k in range(8, bands, 8):
            s = s + a[k : k + 8]
        return s

    def scan(sets):
        zero = jnp.zeros((bands, lanes), f32)
        ratio = WEIGHTS[1] / WEIGHTS[0]
        n = len(sets)

        def up(z, carry):
            carry = list(carry)
            for r in range(rows):
                part = slice(r * bands, (r + 1) * bands)
                for i, (src, a, b, out) in enumerate(sets):
                    u1, u2, a1, a2 = carry[i]
                    e, b1, b2 = src[z, part], a[z, part], b[z, part]
                    u1 = e + (a1 * b1) * u1
                    u2 = ratio * e + (a2 * b2) * u2
                    out[1 + z * rows + r] = fold(u1 + u2)
                    carry[i] = (u1, u2, b1, b2)
            return tuple(carry)

        def down(k, carry):
            carry = list(carry)
            z = walls - 1 - k
            for r in reversed(range(rows)):
                part = slice(r * bands, (r + 1) * bands)
                for i, (src, a, b, out) in enumerate(sets):
                    d1, d2, a1, a2 = carry[i]
                    e, b1, b2 = src[z, part], a[z, part], b[z, part]
                    d1 = e + (a1 * b1) * d1
                    d2 = ratio * e + (a2 * b2) * d2
                    at = 1 + z * rows + r
                    out[at] = out[at] - fold(d1 + d2)
                    carry[i] = (d1, d2, b1, b2)
            return tuple(carry)

        start = ((zero,) * 4,) * n
        loop(walls, up, start)
        ends = loop(walls, down, start)
        for _s, _a, _b, out in sets:
            out[0] = out[1]
            out[total + 1] = out[total]
        d1, d2, a1, a2 = ends[0]
        return jnp.sum(fold(a1 * d1 + a2 * d2), axis=0, keepdims=True)

    sub = lax.broadcasted_iota(jnp.int32, (rows, lanes), 0)

    def heat(ref, z):
        at = z * rows
        a = [ref[at + i] - ref[at + i + 2] for i in range(rows)]
        order = [4 * ((s >> 2) & 1) + 2 * (1 - ((s >> 1) & 1)) + (1 - (s & 1)) for s in range(8)]
        a = [a[order.index(i)] for i in range(8)]
        low = sub < 4
        b = [jnp.where(low, a[i], a[i + 4]) + pltpu.roll(jnp.where(low, a[i + 4], a[i]), 4, 0) for i in range(4)]
        low = (sub & 3) < 2
        c = [
            jnp.where(low, b[i + 2] + pltpu.roll(b[i + 2], rows - 2, 0), b[i] + pltpu.roll(b[i], 2, 0))
            for i in range(2)
        ]
        low = (sub & 1) < 1
        d = jnp.where(low, c[1] + pltpu.roll(c[1], rows - 1, 0), c[0] + pltpu.roll(c[0], 1, 0))
        return heat_scale * d

    def around(x, h):
        s = {0: x}
        for o in (1, 2, 3):
            s[o] = pltpu.roll(jnp.where(lane >= o, x, h), lanes - o, 1)
            s[-o] = pltpu.roll(jnp.where(lane < lanes - o, x, h), o, 1)
        return s

    def tendency(s, cour):
        gradient = (45.0 / 60.0) * (s[1] - s[-1]) - (9.0 / 60.0) * (s[2] - s[-2]) + (1.0 / 60.0) * (s[3] - s[-3])
        smooth = (s[-3] + s[3]) - 6.0 * (s[-2] + s[2]) + 15.0 * (s[-1] + s[1]) - 20.0 * s[0]
        return FILTER * smooth - cour * gradient

    left_half = lane < lanes // 2

    def halo_of(pr, pk, c):
        a = pltpu.roll(pr, lanes - REACH * c, 1) if c else pr
        return jnp.where(left_half, a, pltpu.roll(pk, lanes - REACH * (c + 1), 1))

    def block(z):
        x = gs[z]
        fill(z, x, em, t1, t2, True)
        pr, pk = gr[z], gl[z]
        h = [halo_of(pr, pk, c) for c in range(comps)]
        fill(z, jnp.stack(h), em_h, t1_h, t2_h, True)
        cour = gc[z]
        m = [x[c] + tendency(around(x[c], h[c]), cour) for c in range(comps)]
        m = jnp.stack(m)
        ms[z] = m
        fill(z, m, em_m, t1_m, t2_m, False)

    for i in range(2):

        @pl.when(jnp.logical_not(first[i]))
        def _later():
            pl.semaphore_wait(ready.at[1 + i, me], 1)
            edge_copy(i, 0, me).start()

    loop(walls - 1, send_on, 0)
    for c in edge_copies(0, me):
        c.wait_recv()
    block(me)
    pr, pk = gr[me], gl[me]
    hc = halo_of(pr, pk, comps)
    cour = gc[me]
    for c in range(comps):
        h = halo_of(pr, pk, c)
        x = gs[me, c]
        mh[c] = h + tendency(around(h, x), hc)
        if c:
            m = ms[me, c]
            new_state[c] = 0.5 * (x + m + tendency(around(m, mh[c]), cour))

    def arrive(i, _):
        z = peer(i + 1)
        d = walls - 1 - i
        state_copy(d, z).wait_recv()
        line_copy(d, z).wait_recv()
        for c in edge_copies(d, z):
            c.wait_recv()
        block(z)
        return 0

    lax.fori_loop(0, walls - 1, arrive, 0)
    flux = scan([(em, t1, t2, net), (em_h, t1_h, t2_h, net_h)])

    def middle(z, _):
        m = ms[z, 0] + heat(net, z)
        ms[z, 0] = m
        t = fourth(m)
        for r in range(rows):
            part = slice(r * bands, (r + 1) * bands)
            em_m[z, part] = em_m[z, part] * t[r : r + 1]
        return 0

    loop(walls, middle, 0)
    flux = flux + scan([(em_m, t1_m, t2_m, net)])
    wall_out[...] = 0.5 * flux
    m = ms[me, 0]
    h = mh[0] + heat(net_h, me)
    new_state[0] = 0.5 * (gs[me, 0] + m + tendency(around(m, h), cour) + heat(net, me))

    def finish(i, _):
        nxt = peer(i + 2)

        @pl.when(jnp.logical_not((nxt < me) & (nxt > 0)))
        def _last():
            state_copy(i + 1, me).wait_send()

        line_copy(i + 1, me).wait_send()
        for c in edge_copies(i + 1, me):
            c.wait_send()
        return 0

    loop(walls - 1, finish, 0)
    for c in edge_copies(0, me):
        c.wait_send()


def hand_over(a, b, a_out, b_out, sems):
    copies = [pltpu.make_async_copy(a, a_out, sems.at[0]), pltpu.make_async_copy(b, b_out, sems.at[1])]
    for c in copies:
        c.start()
    for c in copies:
        c.wait()


def local(walls, azims, state, courant, cross_sections, band_fractions, absorb_index, band_index):
    comps, stations, rows, lanes = state.shape
    bands = absorb_index.shape[1]
    species = absorb_index.shape[0]
    entries = cross_sections.shape[0]
    total = rows * walls
    f32 = jnp.float32
    vmem = pltpu.VMEM
    dma = pltpu.SemaphoreType.DMA
    hbm_spec = pl.BlockSpec(memory_space=pltpu.HBM)
    vmem_spec = pl.BlockSpec(memory_space=pltpu.VMEM)
    new_state, wall = pl.pallas_call(
        functools.partial(kernel, walls, azims),
        out_shape=(
            pltpu.VMEM((comps, rows, lanes), f32),
            pltpu.VMEM((1, lanes), f32),
        ),
        in_specs=[hbm_spec] * 6,
        out_specs=(vmem_spec, vmem_spec),
        scratch_shapes=[
            vmem((walls, comps, rows, lanes), f32),
            vmem((walls, rows, lanes), f32),
            vmem((walls, rows, lanes), f32),
            vmem((walls, rows, lanes), f32),
            vmem((walls, comps, rows, lanes), f32),
            vmem((comps, rows, lanes), f32),
            vmem((rows, lanes), f32),
            vmem((rows, lanes), f32),
        ] + [vmem((walls, rows * bands, lanes), f32)] * 9 + [
            vmem((total + 2, 8, lanes), f32),
            vmem((total + 2, 8, lanes), f32),
            vmem((16, lanes), f32),
            vmem((species, bands), jnp.int32),
            pltpu.SMEM((entries,), f32),
            pltpu.SMEM((entries,), f32),
            pltpu.SMEM((bands,), jnp.int32),
            dma((6,)),
        ] + [dma((walls,))] * 4 + [dma((2, walls))] * 2 + [pltpu.SemaphoreType.REGULAR((3, walls))],
        compiler_params=pltpu.CompilerParams(
            collective_id=0, has_side_effects=True, vmem_limit_bytes=58 * 1024 * 1024),
    )(state.reshape(comps, rows, lanes), courant.reshape(rows, lanes), cross_sections, band_fractions, absorb_index, band_index)
    hbm = pl.BlockSpec(memory_space=pltpu.HBM)
    new_state, wall = pl.pallas_call(
        hand_over,
        out_shape=(
            jax.ShapeDtypeStruct((comps, rows, lanes), f32),
            jax.ShapeDtypeStruct((1, lanes), f32),
        ),
        in_specs=[pl.BlockSpec(memory_space=pl.ANY)] * 2,
        out_specs=(hbm, hbm),
        scratch_shapes=[dma((2,))],
    )(pltpu.with_memory_space_constraint(new_state, pltpu.VMEM), pltpu.with_memory_space_constraint(wall, pltpu.VMEM))
    return new_state.reshape(state.shape), wall


def solution(mesh):
    return jax.shard_map(
        functools.partial(local, mesh.shape["wall"], mesh.shape["azim"]),
        mesh=mesh,
        in_specs=(P(None, "case", "wall", "azim"), P("case", "wall", "azim"), P(), P(), P(), P()),
        out_specs=(P(None, "case", "wall", "azim"), P("case", "azim")),
        check_vma=False,
    )
```

time: 15 us -> 13.4 us (0.89)
  the two profiles are of different devices: /device:TPU:0 before, /device:TPU:9 now
where the time goes in v1:
time: 13.4 us; the launch traced here: 13.3 us
  Pallas kernels  12.6 us (94%)
  between operations  0.64 us (5%)
    pallas_call x1, Pallas kernels, local(): pl.pallas_call(functools.partial(kernel, walls, azims), out_shape=(pltpu....  12 us
    pallas_call x1, Pallas kernels, local(): pl.pallas_call(hand_over, out_shape=(jax.ShapeDtypeStruct((comps, rows, l...  0.64 us

profile of v1, /device:TPU:9, one launch (start us, length us, event | category | flops | bytes accessed | tf_op | source)
XLA Modules:
  0.0 13.3 jit_solution(8215119698383710637)
XLA Ops:
  0.6 12.0 %shard_map.77 = (f32[12,8,128]{2,1,0:T(8,128)S(1)}, f32[1,128]{1,0:T(1,128)S(1)}) custom-call(f32[12,8,128]{2,1,0:T(8,128)} %bitcast.5, f32[8,128]{1,0:T(8,128)} %bitcast.6, f32[64]{0:T(128)} %sections.1, f32[64]{0:T(128)} %fractions.1, s32[11,16]{1,0:T(8,128)} %absorb.1, s32[16]{0:T(128)} %band.1), custom_call_target="tpu_custom_call" | custom-call | tf_op jit(solution)/shard_map/pallas_call | solution.py:416
  12.6 0.6 %shard_map.78 = (f32[12,8,128]{2,1,0:T(8,128)}, f32[1,128]{1,0:T(1,128)}) custom-call(f32[12,8,128]{2,1,0:T(8,128)S(1)} %get-tuple-element.6.a, f32[1,128]{1,0:T(1,128)S(1)} %get-tuple-element.7.b), custom_call_target="tpu_custom_call" | custom-call | tf_op jit(solution)/shard_map/pallas_call | solution.py:447

commit v2 on v1

--- a/solution.py
+++ b/solution.py
@@ -29,14 +29,14 @@
     new_state, wall_out,
     gs, gc, gl, gr, ms, mh, edge_l, edge_r,
     em, t1, t2, em_h, t1_h, t2_h, em_m, t1_m, t2_m, net, net_h,
-    table, idx, cs, bf, bi,
+    table, col, idx, cs, bf, bi,
     local_sem, s_state, r_state, s_cour, r_cour, s_edge, r_edge, ready,
 ):
     comps, rows, lanes = state.shape
     species, bands = absorb.shape
     entries = sections.shape[0]
     total = rows * walls
-    f32, bf16 = jnp.float32, jnp.bfloat16
+    f32 = jnp.float32
     me = lax.axis_index("wall")
     az = lax.axis_index("azim")
     right, left = lax.rem(az + 1, azims), lax.rem(az + azims - 1, azims)
@@ -75,21 +75,14 @@
     for c in loads:
         c.start()
 
-    greeters = 3 * me + first[0].astype(jnp.int32) + first[1].astype(jnp.int32)
-
-    @pl.when(greeters > 0)
-    def _greeted():
-        pl.semaphore_wait(barrier, greeters)
-
-
     def state_copy(d, slot):
         return pltpu.make_async_remote_copy(
-            src_ref=state, dst_ref=gs.at[slot], send_sem=s_state.at[d], recv_sem=r_state.at[d],
+            src_ref=gs.at[me], dst_ref=gs.at[slot], send_sem=s_state.at[d], recv_sem=r_state.at[d],
             device_id={"wall": peer(d)}, device_id_type=MESH)
 
     def line_copy(d, slot):
         return pltpu.make_async_remote_copy(
-            src_ref=courant, dst_ref=gc.at[slot], send_sem=s_cour.at[d], recv_sem=r_cour.at[d],
+            src_ref=gc.at[me], dst_ref=gc.at[slot], send_sem=s_cour.at[d], recv_sem=r_cour.at[d],
             device_id={"wall": peer(d)}, device_id_type=MESH)
 
     def edge_copy(i, d, slot):
@@ -101,13 +94,15 @@
     def edge_copies(d, slot):
         return [edge_copy(i, d, slot) for i in range(2)]
 
-    def state_first(i, _):
+    def send_first(i, _):
         z = peer(i + 1)
 
         @pl.when((z < me) & (z == 0))
         def _earliest():
+            line_copy(i + 1, me).start()
+            for c in edge_copies(i + 1, me):
+                c.start()
             state_copy(i + 1, me).start()
-            line_copy(i + 1, me).start()
 
         return 0
 
@@ -127,12 +122,20 @@
 
         @pl.when((z < me) & (z > 0))
         def _earlier():
-            state_copy(i, me).wait_send()
             state_copy(i + 1, me).start()
+
+        return 0
+
+    def edges_back(i, _):
+        z = peer(i + 1)
+
+        @pl.when((z < me) & (z > 0))
+        def _earlier():
+            @pl.when(z == 1)
+            def _paced():
+                state_copy(i, me).wait_send()
+
             line_copy(i + 1, me).start()
-
-        @pl.when(z < me)
-        def _edges():
             for c in edge_copies(i + 1, me):
                 c.start()
 
@@ -144,21 +147,13 @@
         @pl.when(z > me)
         def _later():
             pl.semaphore_wait(ready.at[0, z], 1)
+            line_copy(i + 1, me).start()
             state_copy(i + 1, me).start()
-            line_copy(i + 1, me).start()
             for k in range(2):
                 pl.semaphore_wait(ready.at[1 + k, z], 1)
                 edge_copy(k, i + 1, me).start()
 
         return 0
-
-    loop(walls - 1, state_first, 0)
-    loop(walls - 1, say_ready, 0)
-    for i in range(2):
-
-        @pl.when(first[i])
-        def _earlier():
-            pl.semaphore_signal(ready.at[2 - i, me], inc=1, device_id={"azim": sides[i]}, device_id_type=MESH)
 
     for c in loads[:2]:
         c.wait()
@@ -172,7 +167,20 @@
         er = jnp.where(here, pltpu.roll(x, (REACH * (c + 1)) % lanes, 1), er)
     edge_l[...] = el
     edge_r[...] = er
-    loop(walls - 1, rest_back, 0)
+    greeters = 3 * me + first[0].astype(jnp.int32) + first[1].astype(jnp.int32)
+
+    @pl.when(greeters > 0)
+    def _greeted():
+        pl.semaphore_wait(barrier, greeters)
+
+    loop(walls - 1, send_first, 0)
+    loop(walls - 1, say_ready, 0)
+    for i in range(2):
+
+        @pl.when(first[i])
+        def _earlier():
+            pl.semaphore_signal(ready.at[2 - i, me], inc=1, device_id={"azim": sides[i]}, device_id_type=MESH)
+
     for i in range(2):
 
         @pl.when(first[i])
@@ -187,21 +195,12 @@
         0, entries, lambda t, acc: jnp.where(index == t, cs[t], acc), jnp.zeros((species, bands), f32), unroll=8)
     table[...] = jnp.zeros_like(table)
     table[0:species, 0:bands] = picked
-    kpad = table.shape[0]
-    rb = rows * bands
-    cr = comps * rows
-    spread = jnp.where(
-        lax.broadcasted_iota(jnp.int32, (rb, lanes), 0) & (bands - 1) == lax.broadcasted_iota(jnp.int32, (rb, lanes), 1), 1.0, 0.0)
-    by_row = lax.dot_general(spread, table[...], (((1,), (1,)), ((), ())), precision=EXACT, preferred_element_type=f32)
-    columns = jnp.where(
-        lax.broadcasted_iota(jnp.int32, (kpad, cr), 1) // rows == lax.broadcasted_iota(jnp.int32, (kpad, cr), 0) + 1, 1.0, 0.0)
-    full = jnp.dot(by_row, columns, precision=EXACT, preferred_element_type=f32)
-    same_row = lax.broadcasted_iota(jnp.int32, (rb, cr), 0) // bands == lax.broadcasted_iota(jnp.int32, (rb, cr), 1) % rows
-    mat = jnp.where(same_row, full, 0.0) * (1.0 / total)
-    mat_hi = mat.astype(bf16)
-    mat_lo = (mat - mat_hi.astype(f32)).astype(bf16)
-    mats = jnp.concatenate(
-        [jnp.concatenate([mat_hi, mat_hi], axis=1), jnp.concatenate([mat_lo, mat_lo], axis=1)], axis=0)
+    one_hot = jnp.where(
+        lax.broadcasted_iota(jnp.int32, (bands, lanes), 0) == lax.broadcasted_iota(jnp.int32, (bands, lanes), 1), 1.0, 0.0)
+    by_band = lax.dot_general(one_hot, table[...], (((1,), (1,)), ((), ())), precision=EXACT, preferred_element_type=f32)
+    by_band = by_band * (1.0 / total)
+    for k in range(species):
+        col[k] = jnp.broadcast_to(by_band[:, k : k + 1], (bands, lanes))
     band_row = lax.broadcasted_iota(jnp.int32, (bands, lanes), 0)
     share = jnp.zeros((bands, lanes), f32)
     for b in range(bands):
@@ -209,22 +208,17 @@
     share = share * WEIGHTS[0]
     heat_scale = COUPLING * total / 2.0
 
-    def steps(values):
-        u = values.reshape(cr, lanes)
-        hi = u.astype(bf16)
-        lo = (u - hi.astype(f32)).astype(bf16)
-        both = jnp.dot(mats, jnp.concatenate([hi, lo], axis=0), preferred_element_type=f32)
-        return both[:rb] + both[rb:]
-
     def fill(z, values, to_em, to_1, to_2, hot):
-        step = steps(values)
-        to_1[z] = jnp.exp(step * (-0.5 * RATES[0]))
-        to_2[z] = jnp.exp(step * (-0.5 * RATES[1]))
         if hot:
             t = fourth(values[0])
         for r in range(rows):
             part = slice(r * bands, (r + 1) * bands)
-            to_em[z, part] = step[part] * (share * t[r : r + 1] if hot else share)
+            step = col[0] * values[1][r : r + 1]
+            for k in range(1, species):
+                step = step + col[k] * values[1 + k][r : r + 1]
+            to_1[z, part] = jnp.exp(step * (-0.5 * RATES[0]))
+            to_2[z, part] = jnp.exp(step * (-0.5 * RATES[1]))
+            to_em[z, part] = step * (share * t[r : r + 1] if hot else share)
 
     def fourth(t):
         t = t * t
@@ -319,11 +313,11 @@
         fill(z, x, em, t1, t2, True)
         pr, pk = gr[z], gl[z]
         h = [halo_of(pr, pk, c) for c in range(comps)]
-        fill(z, jnp.stack(h), em_h, t1_h, t2_h, True)
+        fill(z, h, em_h, t1_h, t2_h, True)
         cour = gc[z]
         m = [x[c] + tendency(around(x[c], h[c]), cour) for c in range(comps)]
-        m = jnp.stack(m)
-        ms[z] = m
+        for c in range(comps):
+            ms[z, c] = m[c]
         fill(z, m, em_m, t1_m, t2_m, False)
 
     for i in range(2):
@@ -334,6 +328,8 @@
             edge_copy(i, 0, me).start()
 
     loop(walls - 1, send_on, 0)
+    loop(walls - 1, edges_back, 0)
+    loop(walls - 1, rest_back, 0)
     for c in edge_copies(0, me):
         c.wait_recv()
     block(me)
@@ -380,7 +376,7 @@
     def finish(i, _):
         nxt = peer(i + 2)
 
-        @pl.when(jnp.logical_not((nxt < me) & (nxt > 0)))
+        @pl.when(jnp.logical_not((nxt < me) & (nxt == 1)))
         def _last():
             state_copy(i + 1, me).wait_send()
 
@@ -434,6 +430,7 @@
             vmem((total + 2, 8, lanes), f32),
             vmem((total + 2, 8, lanes), f32),
             vmem((16, lanes), f32),
+            vmem((species, bands, lanes), f32),
             vmem((species, bands), jnp.int32),
             pltpu.SMEM((entries,), f32),
             pltpu.SMEM((entries,), f32),

time: 13.4 us -> 12.9 us (0.963)
  the two profiles are of different devices: /device:TPU:9 before, /device:TPU:25 now
where the time goes in v2:
time: 12.9 us; the launch traced here: 12.7 us
  Pallas kernels  12.1 us (94%)
  between operations  0.64 us (5%)
    pallas_call x1, Pallas kernels, local(): pl.pallas_call(functools.partial(kernel, walls, azims), out_shape=(pltpu....  11.4 us
    pallas_call x1, Pallas kernels, local(): pl.pallas_call(hand_over, out_shape=(jax.ShapeDtypeStruct((comps, rows, l...  0.64 us

profile of v2, /device:TPU:25, one launch (start us, length us, event | category | flops | bytes accessed | tf_op | source)
XLA Modules:
  0.0 12.7 jit_solution(5563129556010508015)
XLA Ops:
  0.6 11.4 %shard_map.77 = (f32[12,8,128]{2,1,0:T(8,128)S(1)}, f32[1,128]{1,0:T(1,128)S(1)}) custom-call(f32[12,8,128]{2,1,0:T(8,128)} %bitcast.5, f32[8,128]{1,0:T(8,128)} %bitcast.6, f32[64]{0:T(128)} %sections.1, f32[64]{0:T(128)} %fractions.1, s32[11,16]{1,0:T(8,128)} %absorb.1, s32[16]{0:T(128)} %band.1), custom_call_target="tpu_custom_call" | custom-call | tf_op jit(solution)/shard_map/pallas_call | solution.py:412
  12.1 0.6 %shard_map.78 = (f32[12,8,128]{2,1,0:T(8,128)}, f32[1,128]{1,0:T(1,128)}) custom-call(f32[12,8,128]{2,1,0:T(8,128)S(1)} %get-tuple-element.6.a, f32[1,128]{1,0:T(1,128)S(1)} %get-tuple-element.7.b), custom_call_target="tpu_custom_call" | custom-call | tf_op jit(solution)/shard_map/pallas_call | solution.py:444

commit v3 on v2

--- a/solution.py
+++ b/solution.py
@@ -12,6 +12,7 @@
 FILTER = 0.02
 COUPLING = 0.1
 REACH = 6
+NEAR = REACH // 2
 MESH = pl.DeviceIdType.MESH
 EXACT = lax.Precision.HIGHEST
 
@@ -29,14 +30,14 @@
     new_state, wall_out,
     gs, gc, gl, gr, ms, mh, edge_l, edge_r,
     em, t1, t2, em_h, t1_h, t2_h, em_m, t1_m, t2_m, net, net_h,
-    table, col, idx, cs, bf, bi,
+    table, col, spread, gather, idx, cs, bf, bi,
     local_sem, s_state, r_state, s_cour, r_cour, s_edge, r_edge, ready,
 ):
     comps, rows, lanes = state.shape
     species, bands = absorb.shape
     entries = sections.shape[0]
     total = rows * walls
-    f32 = jnp.float32
+    f32, bf16 = jnp.float32, jnp.bfloat16
     me = lax.axis_index("wall")
     az = lax.axis_index("azim")
     right, left = lax.rem(az + 1, azims), lax.rem(az + azims - 1, azims)
@@ -160,11 +161,11 @@
     lane = lax.broadcasted_iota(jnp.int32, (rows, lanes), 1)
     el = jnp.zeros((rows, lanes), f32)
     er = jnp.zeros((rows, lanes), f32)
+    lane_r, lane_l = (lane + NEAR) % lanes, (lane + lanes - NEAR) % lanes
     for c in range(comps + 1):
-        x = gs[me, c] if c < comps else gc[me]
-        here = (lane >= REACH * c) & (lane < REACH * (c + 1))
-        el = jnp.where(here, pltpu.roll(x, REACH * c, 1) if c else x, el)
-        er = jnp.where(here, pltpu.roll(x, (REACH * (c + 1)) % lanes, 1), er)
+        x = pltpu.roll(gs[me, c] if c < comps else gc[me], (REACH * c + NEAR) % lanes, 1)
+        el = jnp.where((lane_l >= REACH * c) & (lane_l < REACH * (c + 1)), x, el)
+        er = jnp.where((lane_r >= REACH * c) & (lane_r < REACH * (c + 1)), x, er)
     edge_l[...] = el
     edge_r[...] = er
     greeters = 3 * me + first[0].astype(jnp.int32) + first[1].astype(jnp.int32)
@@ -207,6 +208,25 @@
         share = jnp.where(band_row == b, bf[bi[b]], share)
     share = share * WEIGHTS[0]
     heat_scale = COUPLING * total / 2.0
+    share_h = jnp.zeros((rows, lanes), f32)
+    for b in range(bands):
+        share_h = jnp.where(lane // REACH == b, bf[bi[b]], share_h)
+    share_h = share_h * WEIGHTS[0]
+    here = lax.broadcasted_iota(jnp.int32, (lanes, lanes), 0)
+    there = lax.broadcasted_iota(jnp.int32, (lanes, lanes), 1)
+    kpad = table.shape[0]
+    by_entry = jnp.where(
+        lax.broadcasted_iota(jnp.int32, (lanes, kpad), 0) // REACH == lax.broadcasted_iota(jnp.int32, (lanes, kpad), 1) + 1, 1.0, 0.0)
+    by_place = jnp.dot(by_entry, table[...], precision=EXACT, preferred_element_type=f32)
+    to_place = jnp.where(here == there // REACH, 1.0, 0.0)
+    area = jnp.dot(by_place, to_place, precision=EXACT, preferred_element_type=f32)
+    same = here % REACH == there % REACH
+    area = jnp.where(same, area, 0.0) * (1.0 / total)
+    area_high = area.astype(bf16)
+    spread[:, 0:lanes] = area_high
+    spread[:, lanes : 2 * lanes] = (area - area_high.astype(f32)).astype(bf16)
+    spread[:, 2 * lanes : 3 * lanes] = jnp.where(same & (here < REACH), 1.0, 0.0).astype(bf16)
+    gather[...] = jnp.where((here < REACH * bands) & (here % REACH == (there + NEAR) % lanes), 1.0, 0.0).astype(bf16)
 
     def fill(z, values, to_em, to_1, to_2, hot):
         if hot:
@@ -230,53 +250,99 @@
             s = s + a[k : k + 8]
         return s
 
-    def scan(sets):
+    ratio = WEIGHTS[1] / WEIGHTS[0]
+
+    def scan(src, a, b):
         zero = jnp.zeros((bands, lanes), f32)
-        ratio = WEIGHTS[1] / WEIGHTS[0]
-        n = len(sets)
 
         def up(z, carry):
-            carry = list(carry)
+            u1, u2, a1, a2 = carry
             for r in range(rows):
                 part = slice(r * bands, (r + 1) * bands)
-                for i, (src, a, b, out) in enumerate(sets):
-                    u1, u2, a1, a2 = carry[i]
-                    e, b1, b2 = src[z, part], a[z, part], b[z, part]
-                    u1 = e + (a1 * b1) * u1
-                    u2 = ratio * e + (a2 * b2) * u2
-                    out[1 + z * rows + r] = fold(u1 + u2)
-                    carry[i] = (u1, u2, b1, b2)
-            return tuple(carry)
+                e, b1, b2 = src[z, part], a[z, part], b[z, part]
+                u1 = e + (a1 * b1) * u1
+                u2 = ratio * e + (a2 * b2) * u2
+                net[1 + z * rows + r] = fold(u1 + u2)
+                a1, a2 = b1, b2
+            return u1, u2, a1, a2
 
         def down(k, carry):
-            carry = list(carry)
+            d1, d2, a1, a2 = carry
             z = walls - 1 - k
             for r in reversed(range(rows)):
                 part = slice(r * bands, (r + 1) * bands)
-                for i, (src, a, b, out) in enumerate(sets):
-                    d1, d2, a1, a2 = carry[i]
-                    e, b1, b2 = src[z, part], a[z, part], b[z, part]
-                    d1 = e + (a1 * b1) * d1
-                    d2 = ratio * e + (a2 * b2) * d2
-                    at = 1 + z * rows + r
-                    out[at] = out[at] - fold(d1 + d2)
-                    carry[i] = (d1, d2, b1, b2)
-            return tuple(carry)
-
-        start = ((zero,) * 4,) * n
-        loop(walls, up, start)
-        ends = loop(walls, down, start)
-        for _s, _a, _b, out in sets:
-            out[0] = out[1]
-            out[total + 1] = out[total]
-        d1, d2, a1, a2 = ends[0]
+                e, b1, b2 = src[z, part], a[z, part], b[z, part]
+                d1 = e + (a1 * b1) * d1
+                d2 = ratio * e + (a2 * b2) * d2
+                at = 1 + z * rows + r
+                net[at] = net[at] - fold(d1 + d2)
+                a1, a2 = b1, b2
+            return d1, d2, a1, a2
+
+        loop(walls, up, (zero,) * 4)
+        d1, d2, a1, a2 = loop(walls, down, (zero,) * 4)
+        net[0] = net[1]
+        net[total + 1] = net[total]
         return jnp.sum(fold(a1 * d1 + a2 * d2), axis=0, keepdims=True)
+
+    def halves(a):
+        high = a.astype(bf16).astype(f32)
+        return jnp.concatenate([high, a - high], axis=0).astype(bf16)
+
+    def fill_edge(z, edge):
+        out = jnp.dot(halves(edge), spread[...], preferred_element_type=f32)
+        step = out[:rows, :lanes] + out[rows:, :lanes] + out[:rows, lanes : 2 * lanes]
+        t = fourth(out[:rows, 2 * lanes :] + out[rows:, 2 * lanes :])
+        t1_h[z] = jnp.exp(step * (-0.5 * RATES[0]))
+        t2_h[z] = jnp.exp(step * (-0.5 * RATES[1]))
+        em_h[z] = step * (share_h * t)
+
+    def edge_flux():
+        zero = jnp.zeros((1, lanes), f32)
+
+        def line(z, r):
+            return em_h[z, r : r + 1], t1_h[z, r : r + 1], t2_h[z, r : r + 1]
+
+        def up(z, carry):
+            u1, u2, a1, a2 = carry
+            for r in range(rows):
+                e, b1, b2 = line(z, r)
+                u1 = e + (a1 * b1) * u1
+                u2 = ratio * e + (a2 * b2) * u2
+                net_h[1 + z * rows + r] = u1 + u2
+                a1, a2 = b1, b2
+            return u1, u2, a1, a2
+
+        def down(k, carry):
+            d1, d2, a1, a2 = carry
+            z = walls - 1 - k
+            for r in reversed(range(rows)):
+                e, b1, b2 = line(z, r)
+                d1 = e + (a1 * b1) * d1
+                d2 = ratio * e + (a2 * b2) * d2
+                at = 1 + z * rows + r
+                net_h[at] = net_h[at] - (d1 + d2)
+                a1, a2 = b1, b2
+            return d1, d2, a1, a2
+
+        loop(walls, up, (zero,) * 4)
+        loop(walls, down, (zero,) * 4)
+        net_h[0] = net_h[1]
+        net_h[total + 1] = net_h[total]
+
+    def edge_heat():
+        at = me * rows
+        change = jnp.concatenate([net_h[at + i] - net_h[at + i + 2] for i in range(rows)], axis=0)
+        out = jnp.dot(halves(change), gather[...], preferred_element_type=f32)
+        return heat_scale * (out[:rows] + out[rows:])
 
     sub = lax.broadcasted_iota(jnp.int32, (rows, lanes), 0)
 
     def heat(ref, z):
         at = z * rows
-        a = [ref[at + i] - ref[at + i + 2] for i in range(rows)]
+        return row_sums([ref[at + i] - ref[at + i + 2] for i in range(rows)])
+
+    def row_sums(a):
         order = [4 * ((s >> 2) & 1) + 2 * (1 - ((s >> 1) & 1)) + (1 - (s & 1)) for s in range(8)]
         a = [a[order.index(i)] for i in range(8)]
         low = sub < 4
@@ -303,17 +369,21 @@
         return FILTER * smooth - cour * gradient
 
     left_half = lane < lanes // 2
+    def back(c):
+        return (lanes - REACH * c - NEAR) % lanes
 
     def halo_of(pr, pk, c):
-        a = pltpu.roll(pr, lanes - REACH * c, 1) if c else pr
-        return jnp.where(left_half, a, pltpu.roll(pk, lanes - REACH * (c + 1), 1))
+        return jnp.where(left_half, pltpu.roll(pr, back(c), 1), pltpu.roll(pk, back(c), 1))
+
+    def near_of(z):
+        return jnp.where(lane % REACH < NEAR, gl[z], gr[z])
 
     def block(z):
         x = gs[z]
         fill(z, x, em, t1, t2, True)
-        pr, pk = gr[z], gl[z]
-        h = [halo_of(pr, pk, c) for c in range(comps)]
-        fill(z, h, em_h, t1_h, t2_h, True)
+        edge = near_of(z)
+        h = [pltpu.roll(edge, back(c), 1) for c in range(comps)]
+        fill_edge(z, edge)
         cour = gc[z]
         m = [x[c] + tendency(around(x[c], h[c]), cour) for c in range(comps)]
         for c in range(comps):
@@ -344,9 +414,15 @@
             m = ms[me, c]
             new_state[c] = 0.5 * (x + m + tendency(around(m, mh[c]), cour))
 
+    def turn(i):
+        if walls != 4:
+            return peer(i + 1)
+        turns = jnp.where(me == 0, 39, jnp.where(me == 1, 44, jnp.where(me == 2, 28, 18)))
+        return (turns >> (2 * i)) & 3
+
     def arrive(i, _):
-        z = peer(i + 1)
-        d = walls - 1 - i
+        z = turn(i)
+        d = lax.rem(me - z + walls, walls)
         state_copy(d, z).wait_recv()
         line_copy(d, z).wait_recv()
         for c in edge_copies(d, z):
@@ -355,7 +431,8 @@
         return 0
 
     lax.fori_loop(0, walls - 1, arrive, 0)
-    flux = scan([(em, t1, t2, net), (em_h, t1_h, t2_h, net_h)])
+    flux = scan(em, t1, t2)
+    edge_flux()
 
     def middle(z, _):
         m = ms[z, 0] + heat(net, z)
@@ -367,10 +444,10 @@
         return 0
 
     loop(walls, middle, 0)
-    flux = flux + scan([(em_m, t1_m, t2_m, net)])
+    flux = flux + scan(em_m, t1_m, t2_m)
     wall_out[...] = 0.5 * flux
     m = ms[me, 0]
-    h = mh[0] + heat(net_h, me)
+    h = mh[0] + edge_heat()
     new_state[0] = 0.5 * (gs[me, 0] + m + tendency(around(m, h), cour) + heat(net, me))
 
     def finish(i, _):
@@ -426,11 +503,14 @@
             vmem((comps, rows, lanes), f32),
             vmem((rows, lanes), f32),
             vmem((rows, lanes), f32),
-        ] + [vmem((walls, rows * bands, lanes), f32)] * 9 + [
+        ] + [vmem((walls, rows * bands, lanes), f32)] * 3 + [vmem((walls, rows, lanes), f32)] * 3 + [
+            vmem((walls, rows * bands, lanes), f32)] * 3 + [
             vmem((total + 2, 8, lanes), f32),
-            vmem((total + 2, 8, lanes), f32),
+            vmem((total + 2, 1, lanes), f32),
             vmem((16, lanes), f32),
             vmem((species, bands, lanes), f32),
+            vmem((lanes, 3 * lanes), jnp.bfloat16),
+            vmem((lanes, lanes), jnp.bfloat16),
             vmem((species, bands), jnp.int32),
             pltpu.SMEM((entries,), f32),
             pltpu.SMEM((entries,), f32),

time: 12.9 us -> 12.6 us (0.977)
  Pallas kernels: 12.1 us -> 11.8 us
    pallas_call x1, Pallas kernels: 11.4 us -> 11.2 us  [local(): pl.pallas_call(functools.partial(kernel, walls, azims), out_shape=(pltpu....]
where the time goes in v3:
time: 12.6 us; the launch traced here: 12.5 us
  Pallas kernels  11.8 us (94%)
  between operations  0.64 us (5%)
    pallas_call x1, Pallas kernels, local(): pl.pallas_call(functools.partial(kernel, walls, azims), out_shape=(pltpu....  11.2 us
    pallas_call x1, Pallas kernels, local(): pl.pallas_call(hand_over, out_shape=(jax.ShapeDtypeStruct((comps, rows, l...  0.64 us

profile of v3, /device:TPU:25, one launch (start us, length us, event | category | flops | bytes accessed | tf_op | source)
XLA Modules:
  0.0 12.5 jit_solution(1995996273724231818)
XLA Ops:
  0.6 11.2 %shard_map.77 = (f32[12,8,128]{2,1,0:T(8,128)S(1)}, f32[1,128]{1,0:T(1,128)S(1)}) custom-call(f32[12,8,128]{2,1,0:T(8,128)} %bitcast.5, f32[8,128]{1,0:T(8,128)} %bitcast.6, f32[64]{0:T(128)} %sections.1, f32[64]{0:T(128)} %fractions.1, s32[11,16]{1,0:T(8,128)} %absorb.1, s32[16]{0:T(128)} %band.1), custom_call_target="tpu_custom_call" | custom-call | tf_op jit(solution)/shard_map/pallas_call | solution.py:489
  11.8 0.6 %shard_map.78 = (f32[12,8,128]{2,1,0:T(8,128)}, f32[1,128]{1,0:T(1,128)}) custom-call(f32[12,8,128]{2,1,0:T(8,128)S(1)} %get-tuple-element.6.a, f32[1,128]{1,0:T(1,128)S(1)} %get-tuple-element.7.b), custom_call_target="tpu_custom_call" | custom-call | tf_op jit(solution)/shard_map/pallas_call | solution.py:524

commit v4 on v3

--- a/solution.py
+++ b/solution.py
@@ -149,10 +149,18 @@
         def _later():
             pl.semaphore_wait(ready.at[0, z], 1)
             line_copy(i + 1, me).start()
-            state_copy(i + 1, me).start()
+
+            @pl.when(z < walls - 1)
+            def _state():
+                state_copy(i + 1, me).start()
+
             for k in range(2):
                 pl.semaphore_wait(ready.at[1 + k, z], 1)
                 edge_copy(k, i + 1, me).start()
+
+            @pl.when(z == walls - 1)
+            def _last():
+                state_copy(i + 1, me).start()
 
         return 0
 
@@ -400,20 +408,6 @@
     loop(walls - 1, send_on, 0)
     loop(walls - 1, edges_back, 0)
     loop(walls - 1, rest_back, 0)
-    for c in edge_copies(0, me):
-        c.wait_recv()
-    block(me)
-    pr, pk = gr[me], gl[me]
-    hc = halo_of(pr, pk, comps)
-    cour = gc[me]
-    for c in range(comps):
-        h = halo_of(pr, pk, c)
-        x = gs[me, c]
-        mh[c] = h + tendency(around(h, x), hc)
-        if c:
-            m = ms[me, c]
-            new_state[c] = 0.5 * (x + m + tendency(around(m, mh[c]), cour))
-
     def turn(i):
         if walls != 4:
             return peer(i + 1)
@@ -421,18 +415,37 @@
         return (turns >> (2 * i)) & 3
 
     def arrive(i, _):
-        z = turn(i)
+        z = jnp.where(i == 0, me, turn(jnp.maximum(i - 1, 0)))
         d = lax.rem(me - z + walls, walls)
-        state_copy(d, z).wait_recv()
-        line_copy(d, z).wait_recv()
+
+        @pl.when(i > 0)
+        def _other():
+            state_copy(d, z).wait_recv()
+            line_copy(d, z).wait_recv()
+
         for c in edge_copies(d, z):
             c.wait_recv()
         block(z)
-        return 0
-
-    lax.fori_loop(0, walls - 1, arrive, 0)
+
+        @pl.when(i == 0)
+        def _own():
+            pr, pk = gr[me], gl[me]
+            hc = halo_of(pr, pk, comps)
+            cour = gc[me]
+            for c in range(comps):
+                h = halo_of(pr, pk, c)
+                x = gs[me, c]
+                mh[c] = h + tendency(around(h, x), hc)
+                if c:
+                    m = ms[me, c]
+                    new_state[c] = 0.5 * (x + m + tendency(around(m, mh[c]), cour))
+
+        return 0
+
+    lax.fori_loop(0, walls, arrive, 0)
+    edge_flux()
     flux = scan(em, t1, t2)
-    edge_flux()
+    heat_h = edge_heat()
 
     def middle(z, _):
         m = ms[z, 0] + heat(net, z)
@@ -446,8 +459,9 @@
     loop(walls, middle, 0)
     flux = flux + scan(em_m, t1_m, t2_m)
     wall_out[...] = 0.5 * flux
+    cour = gc[me]
     m = ms[me, 0]
-    h = mh[0] + edge_heat()
+    h = mh[0] + heat_h
     new_state[0] = 0.5 * (gs[me, 0] + m + tendency(around(m, h), cour) + heat(net, me))
 
     def finish(i, _):

time: 12.6 us -> 12.3 us (0.976)
  the two profiles are of different devices: /device:TPU:25 before, /device:TPU:0 now
where the time goes in v4:
time: 12.3 us; the launch traced here: 12.2 us
  Pallas kernels  11.5 us (93%)
  between operations  0.64 us (5%)
    pallas_call x1, Pallas kernels, local(): pl.pallas_call(functools.partial(kernel, walls, azims), out_shape=(pltpu....  10.9 us
    pallas_call x1, Pallas kernels, local(): pl.pallas_call(hand_over, out_shape=(jax.ShapeDtypeStruct((comps, rows, l...  0.64 us

profile of v4, /device:TPU:0, one launch (start us, length us, event | category | flops | bytes accessed | tf_op | source)
XLA Modules:
  0.0 12.2 jit_solution(13370993987064584495)
XLA Ops:
  0.6 10.9 %shard_map.77 = (f32[12,8,128]{2,1,0:T(8,128)S(1)}, f32[1,128]{1,0:T(1,128)S(1)}) custom-call(f32[12,8,128]{2,1,0:T(8,128)} %bitcast.5, f32[8,128]{1,0:T(8,128)} %bitcast.6, f32[64]{0:T(128)} %sections.1, f32[64]{0:T(128)} %fractions.1, s32[11,16]{1,0:T(8,128)} %absorb.1, s32[16]{0:T(128)} %band.1), custom_call_target="tpu_custom_call" | custom-call | tf_op jit(solution)/shard_map/pallas_call | solution.py:503
  11.5 0.6 %shard_map.78 = (f32[12,8,128]{2,1,0:T(8,128)}, f32[1,128]{1,0:T(1,128)}) custom-call(f32[12,8,128]{2,1,0:T(8,128)S(1)} %get-tuple-element.6.a, f32[1,128]{1,0:T(1,128)S(1)} %get-tuple-element.7.b), custom_call_target="tpu_custom_call" | custom-call | tf_op jit(solution)/shard_map/pallas_call | solution.py:538

commit v5 on v4

--- a/solution.py
+++ b/solution.py
@@ -29,7 +29,7 @@
     walls, azims, state, courant, sections, fractions, absorb, band,
     new_state, wall_out,
     gs, gc, gl, gr, ms, mh, edge_l, edge_r,
-    em, t1, t2, em_h, t1_h, t2_h, em_m, t1_m, t2_m, net, net_h,
+    em, t1, t2, em_h, t1_h, t2_h, em_m, t1_m, t2_m, first_t, first_m, net, net_h,
     table, col, spread, gather, idx, cs, bf, bi,
     local_sem, s_state, r_state, s_cour, r_cour, s_edge, r_edge, ready,
 ):
@@ -103,6 +103,27 @@
             line_copy(i + 1, me).start()
             for c in edge_copies(i + 1, me):
                 c.start()
+
+            @pl.when(jnp.logical_not((me == walls - 1) | ((me == 1) & (az % 2 == 1))))
+            def _at_once():
+                state_copy(i + 1, me).start()
+
+        return 0
+
+    def send_next(i, _):
+        z = peer(i + 1)
+
+        @pl.when((z < me) & (z == 0) & (me == walls - 1))
+        def _after():
+            state_copy(i + 1, me).start()
+
+        return 0
+
+    def send_late(i, _):
+        z = peer(i + 1)
+
+        @pl.when((z < me) & (z == 0) & (me < walls - 1) & ((me == 1) & (az % 2 == 1)))
+        def _late():
             state_copy(i + 1, me).start()
 
         return 0
@@ -197,6 +218,7 @@
             edge_copy(i, 0, me).start()
 
 
+    loop(walls - 1, send_next, 0)
     for c in loads[2:]:
         c.wait()
     index = idx[...]
@@ -236,7 +258,7 @@
     spread[:, 2 * lanes : 3 * lanes] = jnp.where(same & (here < REACH), 1.0, 0.0).astype(bf16)
     gather[...] = jnp.where((here < REACH * bands) & (here % REACH == (there + NEAR) % lanes), 1.0, 0.0).astype(bf16)
 
-    def fill(z, values, to_em, to_1, to_2, hot):
+    def fill(z, values, to_em, to_1, to_2, to_first, hot):
         if hot:
             t = fourth(values[0])
         for r in range(rows):
@@ -244,9 +266,17 @@
             step = col[0] * values[1][r : r + 1]
             for k in range(1, species):
                 step = step + col[k] * values[1 + k][r : r + 1]
-            to_1[z, part] = jnp.exp(step * (-0.5 * RATES[0]))
-            to_2[z, part] = jnp.exp(step * (-0.5 * RATES[1]))
+            half = [jnp.exp(step * (-0.5 * rate)) for rate in RATES]
+            if r:
+                for i, to in enumerate((to_1, to_2)):
+                    to[z, (r - 1) * bands : r * bands] = last[i] * half[i]
+            else:
+                for i in range(2):
+                    to_first[z, i] = half[i]
+            last = half
             to_em[z, part] = step * (share * t[r : r + 1] if hot else share)
+        for i, to in enumerate((to_1, to_2)):
+            to[z, (rows - 1) * bands : rows * bands] = last[i]
 
     def fourth(t):
         t = t * t
@@ -260,32 +290,35 @@
 
     ratio = WEIGHTS[1] / WEIGHTS[0]
 
-    def scan(src, a, b):
+    def scan(src, a, b, head):
         zero = jnp.zeros((bands, lanes), f32)
+
+        def part(r):
+            return slice(r * bands, (r + 1) * bands)
 
         def up(z, carry):
             u1, u2, a1, a2 = carry
             for r in range(rows):
-                part = slice(r * bands, (r + 1) * bands)
-                e, b1, b2 = src[z, part], a[z, part], b[z, part]
-                u1 = e + (a1 * b1) * u1
-                u2 = ratio * e + (a2 * b2) * u2
+                e = src[z, part(r)]
+                k1 = a[z, part(r - 1)] if r else a1 * head[z, 0]
+                k2 = b[z, part(r - 1)] if r else a2 * head[z, 1]
+                u1 = e + k1 * u1
+                u2 = ratio * e + k2 * u2
                 net[1 + z * rows + r] = fold(u1 + u2)
-                a1, a2 = b1, b2
-            return u1, u2, a1, a2
+            return u1, u2, a[z, part(rows - 1)], b[z, part(rows - 1)]
 
         def down(k, carry):
             d1, d2, a1, a2 = carry
             z = walls - 1 - k
             for r in reversed(range(rows)):
-                part = slice(r * bands, (r + 1) * bands)
-                e, b1, b2 = src[z, part], a[z, part], b[z, part]
-                d1 = e + (a1 * b1) * d1
-                d2 = ratio * e + (a2 * b2) * d2
+                e, k1, k2 = src[z, part(r)], a[z, part(r)], b[z, part(r)]
+                if r == rows - 1:
+                    k1, k2 = k1 * a1, k2 * a2
+                d1 = e + k1 * d1
+                d2 = ratio * e + k2 * d2
                 at = 1 + z * rows + r
                 net[at] = net[at] - fold(d1 + d2)
-                a1, a2 = b1, b2
-            return d1, d2, a1, a2
+            return d1, d2, head[z, 0], head[z, 1]
 
         loop(walls, up, (zero,) * 4)
         d1, d2, a1, a2 = loop(walls, down, (zero,) * 4)
@@ -388,7 +421,7 @@
 
     def block(z):
         x = gs[z]
-        fill(z, x, em, t1, t2, True)
+        fill(z, x, em, t1, t2, first_t, True)
         edge = near_of(z)
         h = [pltpu.roll(edge, back(c), 1) for c in range(comps)]
         fill_edge(z, edge)
@@ -396,7 +429,7 @@
         m = [x[c] + tendency(around(x[c], h[c]), cour) for c in range(comps)]
         for c in range(comps):
             ms[z, c] = m[c]
-        fill(z, m, em_m, t1_m, t2_m, False)
+        fill(z, m, em_m, t1_m, t2_m, first_m, False)
 
     for i in range(2):
 
@@ -405,6 +438,7 @@
             pl.semaphore_wait(ready.at[1 + i, me], 1)
             edge_copy(i, 0, me).start()
 
+    loop(walls - 1, send_late, 0)
     loop(walls - 1, send_on, 0)
     loop(walls - 1, edges_back, 0)
     loop(walls - 1, rest_back, 0)
@@ -444,7 +478,7 @@
 
     lax.fori_loop(0, walls, arrive, 0)
     edge_flux()
-    flux = scan(em, t1, t2)
+    flux = scan(em, t1, t2, first_t)
     heat_h = edge_heat()
 
     def middle(z, _):
@@ -457,7 +491,7 @@
         return 0
 
     loop(walls, middle, 0)
-    flux = flux + scan(em_m, t1_m, t2_m)
+    flux = flux + scan(em_m, t1_m, t2_m, first_m)
     wall_out[...] = 0.5 * flux
     cour = gc[me]
     m = ms[me, 0]
@@ -518,7 +552,7 @@
             vmem((rows, lanes), f32),
             vmem((rows, lanes), f32),
         ] + [vmem((walls, rows * bands, lanes), f32)] * 3 + [vmem((walls, rows, lanes), f32)] * 3 + [
-            vmem((walls, rows * bands, lanes), f32)] * 3 + [
+            vmem((walls, rows * bands, lanes), f32)] * 3 + [vmem((walls, 2, bands, lanes), f32)] * 2 + [
             vmem((total + 2, 8, lanes), f32),
             vmem((total + 2, 1, lanes), f32),
             vmem((16, lanes), f32),

time: 12.3 us -> 12.2 us (level)
    pallas_call x1, Pallas kernels: 10.9 us -> 10.7 us  [local(): pl.pallas_call(functools.partial(kernel, walls, azims), out_shape=(pltpu....]
where the time goes in v5:
time: 12.2 us; the launch traced here: 12 us
  Pallas kernels  11.4 us (93%)
  between operations  0.64 us (5%)
    pallas_call x1, Pallas kernels, local(): pl.pallas_call(functools.partial(kernel, walls, azims), out_shape=(pltpu....  10.7 us
    pallas_call x1, Pallas kernels, local(): pl.pallas_call(hand_over, out_shape=(jax.ShapeDtypeStruct((comps, rows, l...  0.64 us

profile of v5, /device:TPU:0, one launch (start us, length us, event | category | flops | bytes accessed | tf_op | source)
XLA Modules:
  0.0 12.0 jit_solution(7529380158398168165)
XLA Ops:
  0.6 10.7 %shard_map.77 = (f32[12,8,128]{2,1,0:T(8,128)S(1)}, f32[1,128]{1,0:T(1,128)S(1)}) custom-call(f32[12,8,128]{2,1,0:T(8,128)} %bitcast.5, f32[8,128]{1,0:T(8,128)} %bitcast.6, f32[64]{0:T(128)} %sections.1, f32[64]{0:T(128)} %fractions.1, s32[11,16]{1,0:T(8,128)} %absorb.1, s32[16]{0:T(128)} %band.1), custom_call_target="tpu_custom_call" | custom-call | tf_op jit(solution)/shard_map/pallas_call | solution.py:537
  11.4 0.6 %shard_map.78 = (f32[12,8,128]{2,1,0:T(8,128)}, f32[1,128]{1,0:T(1,128)}) custom-call(f32[12,8,128]{2,1,0:T(8,128)S(1)} %get-tuple-element.6.a, f32[1,128]{1,0:T(1,128)S(1)} %get-tuple-element.7.b), custom_call_target="tpu_custom_call" | custom-call | tf_op jit(solution)/shard_map/pallas_call | solution.py:572
